TPU v7x, 512 devices: a whole 4x8x8 slice. The times are simulated.
512 devices in a mesh: dp: 4 (over z_hi), segment: 16 (over y, core), patch: 8 (over x, z_lo).
Axes of the slice: x: 4, y: 8, z: 8 (z_hi: 4, z_lo: 2; z = z_hi * 2 + z_lo), core: 2. Of those that a mesh axis runs over, the one named last changes fastest.
Arguments:
- hidden: bfloat16 [64, 1024, 1536], P(('dp', 'segment'), 'patch'), parts along dimension 0, may hold values from -6 to 6
- w_qkv: bfloat16 [16, 1536, 4608], P('segment', None, 'patch'), may hold values from -0.12552947 to 0.12552947
- norm_gain: float32 [16, 1536], P('segment'), may hold values from 0.5 to 1.5
- box_vec: float32 [16, 1536], P('segment'), may hold values from -4 to 4
- gate: float32 [64, 1536], P(('dp', 'segment')), parts along dimension 0, may hold values from 4 to 16
- box_mask: int32 [64, 1024], P(('dp', 'segment'), 'patch'), parts along dimension 0, may hold values 0 or 1
- stale_kv: bfloat16 [64, 2, 1024, 1536], P(('dp', 'segment'), None, 'patch'), parts along dimension 0, may hold values from -6 to 6
Outputs:
- hidden_out: bfloat16 [64, 1024, 1536], P(('dp', 'segment'), 'patch'), parts along dimension 0
- fresh_kv: bfloat16 [64, 2, 1024, 1536], P(('dp', 'segment'), None, 'patch'), parts along dimension 0
There are 4 independent parts, one for each index of `dp`. A program takes and returns all parts, laid end to end along the dimension named above; an argument that names none is the same for every part. Nothing has to cross between parts.
All inputs are finite; a program needn't handle non-finite values. No bound on the sum of `box_mask` on one device may be relied on, other than what follows from the above.
Results may differ from a plain program's by a relative error of at most 0.023.
Values may be sent and summed in bfloat16 or wider, within the bound.
No kernel may reach another device: no remote copies, remote signals or barrier semaphores. Data moves between devices by JAX's collectives and lax.ppermute only.
A program may use at most 64 MiB of HBM per device.

v0:
```python
import jax
import jax.numpy as jnp
from jax import lax
from jax.sharding import PartitionSpec as P

HEADS = 12
HEAD_DIM = 128


def from_behind(shard, axis, by):
    count = lax.axis_size(axis)
    return lax.ppermute(shard, axis, [(i, (i + by) % count) for i in range(count)])


def partial_attention(queries, keys, values):
    count = queries.shape[0]
    length = keys.shape[0]
    qh = queries.reshape(count, HEADS, HEAD_DIM)
    kh = keys.reshape(length, HEADS, HEAD_DIM)
    vh = values.reshape(length, HEADS, HEAD_DIM)
    scores = jnp.einsum("nhd,thd->nht", qh, kh, preferred_element_type=jnp.float32) * HEAD_DIM ** (
        -0.5
    )
    top = jnp.max(scores, axis=-1)
    weights = jnp.exp(scores - top[..., None])
    total = jnp.sum(weights, axis=-1)
    summed = jnp.einsum(
        "nht,thd->nhd", weights.astype(jnp.bfloat16), vh, preferred_element_type=jnp.float32
    )
    return (summed.reshape(count, HEADS * HEAD_DIM), top, total)


def local(hidden, w_qkv, norm_gain, box_vec, gate, box_mask, stale_kv):
    state = hidden[0].astype(jnp.float32)
    rows = state.shape[0]
    width = HEADS * HEAD_DIM
    inverse = lax.rsqrt(jnp.mean(state * state, axis=-1, keepdims=True) + 1e-06)
    normed = (
        state * inverse * norm_gain[0] + box_mask[0][:, None].astype(jnp.float32) * box_vec[0]
    ).astype(jnp.bfloat16)
    weight = w_qkv[0]
    columns = jnp.dot(
        lax.all_gather(normed, "patch", axis=0, tiled=True),
        weight,
        preferred_element_type=jnp.float32,
    ).astype(jnp.bfloat16)
    qkv = lax.all_to_all(columns, "patch", split_axis=0, concat_axis=1, tiled=True)
    queries = qkv[:, :width]
    keys_new = qkv[:, width : 2 * width]
    values_new = qkv[:, 2 * width :]
    fresh = jnp.stack([keys_new, values_new])
    own_start = lax.axis_index("patch") * rows
    whole = lax.all_gather(stale_kv[0], "patch", axis=1, tiled=True)
    whole = lax.dynamic_update_slice_in_dim(whole, fresh, own_start, 1)
    summed, top, total = partial_attention(queries, whole[0], whole[1])
    attended = (summed.reshape(rows, HEADS, HEAD_DIM) / total[..., None]).reshape(rows, width)
    updated = (state + gate[0] * attended).astype(jnp.bfloat16)
    passed = from_behind(updated[None], "segment", 1)
    return (passed, fresh[None])


def solution(mesh):
    placed = (
        P(("dp", "segment"), "patch", None),
        P("segment", None, "patch"),
        P("segment", None),
        P("segment", None),
        P(("dp", "segment"), None),
        P(("dp", "segment"), "patch"),
        P(("dp", "segment"), None, "patch", None),
    )
    return jax.shard_map(
        local,
        mesh=mesh,
        in_specs=placed,
        out_specs=(P(("dp", "segment"), "patch", None), P(("dp", "segment"), None, "patch", None)),
        check_vma=False,
    )
```

profile of v0, /device:TPU:2, one launch (start us, length us, event | category | flops | bytes accessed | tf_op | source)
XLA Modules:
  0.0 266.6 jit_solution(11302217391138647032)
XLA Ops:
  7.2 0.0 copy-start
  7.2 0.0 all-gather.4.cloned.1.call-start
  7.2 0.8 reduce.1
  8.1 0.7 reduce.2
  8.8 1.2 fusion.23
  9.9 0.7 convert_bitcast_fusion.1
  10.6 2.0 fusion.26
  12.6 0.0 all-gather.4.cloned.1.call-update
  12.6 0.0 all-gather.6.cloned.1.call-start
  12.7 2.3 copy.13
  15.0 0.0 all-gather.6.cloned.1.call-update
  15.0 78.0 %all-gather.4.cloned.1.call-done = bf16[1024,1536]{1,0:T(8,128)(2,1)} async-done(((bf16[128,1536]{1,0:T(8,128)(2,1)}), bf16[1024,1536]{1,0:T(8,128)(2,1)}) %all-gather.4.cloned.1.call-update) | async-done | bytes 3145744 | tf_op jit(solution)/shard_map/all_gather | solution.py:43
  93.0 0.0 copy-done
  93.0 3.9 %fusion.12 = bf16[72,8,8,128]{3,2,1,0:T(8,128)(2,1)S(1)} fusion(bf16[1024,1536]{1,0:T(8,128)(2,1)} %all-gather.4.cloned.1.call-done, bf16[1,1536,576]{1,2,0:T(8,128)(2,1)S(1)} %copy-done), kind=kOutput, calls=%fused_computation.11 | convolution fusion | flops 1812529152 | bytes 6094848 | tf_op jit(solution)/shard_map/dot_general | solution.py:42
  96.9 0.0 copy-start.2
  96.9 1.3 copy.25
  98.2 5.4 %all-to-all-start = ((bf16[8,128,576]{1,2,0:T(8,128)(2,1)}), bf16[8,128,576]{1,2,0:T(8,128)(2,1)S(1)}, u32[]{:S(2)}, u32[]{:S(2)}) async-start(bf16[8,128,576]{1,2,0:T(8,128)(2,1)} %bitcast.67), calls=%async_computation | async-start | bytes 2359296 | tf_op jit(solution)/shard_map/all_to_all | solution.py:47
  103.5 21.3 %all-to-all-done = bf16[8,128,576]{1,2,0:T(8,128)(2,1)S(1)} async-done(((bf16[8,128,576]{1,2,0:T(8,128)(2,1)}), bf16[8,128,576]{1,2,0:T(8,128)(2,1)S(1)}, u32[]{:S(2)}, u32[]{:S(2)}) %all-to-all-start) | async-done | bytes 1179680 | tf_op jit(solution)/shard_map/all_to_all | solution.py:47
  124.9 1.0 fusion.32
  125.9 110.5 %all-gather.6.cloned.1.call-done = bf16[1,2,1024,1536]{2,3,1,0:T(8,128)(2,1)} async-done(((bf16[1,2,128,1536]{2,3,1,0:T(8,128)(2,1)}), bf16[1,2,1024,1536]{2,3,1,0:T(8,128)(2,1)}) %all-gather.6.cloned.1.call-update) | async-done | bytes 6291472 | tf_op jit(solution)/shard_map/all_gather | solution.py:53
  236.3 2.3 fusion.28
  238.7 3.6 %fusion.31 = (bf16[1,1024,1536]{1,2,0:T(8,128)(2,1)S(1)}, bf16[1,1024,1536]{1,2,0:T(8,128)(2,1)S(1)}) fusion(bf16[2,1024,1536]{1,2,0:T(8,128)(2,1)} %get-tuple-element.10), kind=kLoop, calls=%fused_computation.32 | loop fusion | bytes 12582912 | tf_op jit(solution)/shard_map/slice | solution.py:55
  242.2 1.3 bitcast_reduce_fusion
  243.5 1.0 fusion.1
  244.5 0.0 copy-start.1
  244.6 2.6 fusion.20
  247.1 2.3 copy.18
  249.4 1.2 fusion.27
  250.6 0.1 collective-permute-start
  250.7 1.2 copy.19
  251.9 7.2 %collective-permute-done = bf16[1,128,1536]{2,1,0:T(8,128)(2,1)S(1)} collective-permute-done((bf16[1,128,1536]{2,1,0:T(8,128)(2,1)S(1)}, bf16[1,128,1536]{2,1,0:T(8,128)(2,1)S(1)}, u32[]{:S(2)}, u32[]{:S(2)}) %collective-permute-start) | collective-permute-done | bytes 393248 | tf_op jit(solution)/shard_map/ppermute | solution.py:12
  259.1 0.7 copy.28
  (4 shorter events, 0.0 us)
Async XLA Ops:
  7.2 85.8 %copy-start = (bf16[1,1536,576]{1,2,0:T(8,128)(2,1)S(1)}, bf16[1,1536,576]{1,2,0:T(8,128)(2,1)}, u32[]{:S(2)}) copy-start(bf16[1,1536,576]{1,2,0:T(8,128)(2,1)} %param.8) | copy-start | bytes 5308420
  7.2 85.8 %all-gather.4.cloned.1.call-start = ((), (), s32[]{:S(2)}) async-start(), calls=%async_computation.1 | async-start | bytes 3538944 | tf_op jit(solution)/shard_map/all_gather | solution.py:43
  12.6 223.7 %all-gather.6.cloned.1.call-start = ((), (), s32[]{:S(2)}) async-start(), calls=%async_computation.2 | async-start | bytes 7077888 | tf_op jit(solution)/shard_map/all_gather | solution.py:53
  96.9 6.6 %copy-start.2 = (f32[1,1536]{1,0:T(1,128)S(1)}, f32[1,1536]{1,0:T(1,128)}, u32[]{:S(2)}) copy-start(f32[1,1536]{1,0:T(1,128)} %param.11) | copy-start | bytes 18436
  98.2 26.7 %all-to-all-start = ((bf16[8,128,576]{1,2,0:T(8,128)(2,1)}), bf16[8,128,576]{1,2,0:T(8,128)(2,1)S(1)}, u32[]{:S(2)}, u32[]{:S(2)}) async-start(bf16[8,128,576]{1,2,0:T(8,128)(2,1)} %bitcast.67), calls=%async_computation | async-start | bytes 2359296 | tf_op jit(solution)/shard_map/all_to_all | solution.py:47
  244.5 4.9 %copy-start.1 = (bf16[1,128,1536]{2,1,0:T(8,128)(2,1)S(1)}, bf16[1,128,1536]{2,1,0:T(8,128)(2,1)}, u32[]{:S(2)}) copy-start(bf16[1,128,1536]{2,1,0:T(8,128)(2,1)} %param.7) | copy-start | bytes 1179652
  250.6 8.4 %collective-permute-start = (bf16[1,128,1536]{2,1,0:T(8,128)(2,1)S(1)}, bf16[1,128,1536]{2,1,0:T(8,128)(2,1)S(1)}, u32[]{:S(2)}, u32[]{:S(2)}) collective-permute-start(bf16[1,128,1536]{2,1,0:T(8,128)(2,1)S(1)} %fusion.27), channel_id=1, source_target_pairs={{0,8},{8,16},{16,24},{24,32},{32,40},{40,48},{48,56},{56,64},{64,7... | collective-permute-start | bytes 1179656 | tf_op jit(solution)/shard_map/ppermute | solution.py:12
Sparse Core Ops, SparseCore 0:
  12.7 80.1 all-gather.3
  95.6 140.7 all-gather.5
where the time goes:
time: 267 us
  waiting for transfers between devices  217 us (81%)
  between operations  14.1 us (5%)
  local copies, waits for them, and re-layouts  12.3 us (5%)
  other arithmetic  9.98 us (4%)
  matrix products  7.76 us (3%)
  starting transfers between devices  5.51 us (2%)
    all_gather x1, waiting for transfers between devices, local(): whole = lax.all_gather(stale_kv[0], 'patch', axis=1, tiled=True)  110 us
    all_gather x1, waiting for transfers between devices, local(): lax.all_gather(normed, 'patch', axis=0, tiled=True)  78 us
    all_to_all x1, waiting for transfers between devices, local(): lax.all_to_all(columns, 'patch', split_axis=0, concat_axis=1, tiled=True)  21.3 us
    ppermute x1, waiting for transfers between devices, from_behind(): lax.ppermute(shard, axis, [(i, (i + by) % count) for i in range(count)])  7.2 us
    all_to_all x1, starting transfers between devices, local(): lax.all_to_all(columns, 'patch', split_axis=0, concat_axis=1, tiled=True)  5.36 us
  transfers between devices with their start and end apart: 4, of which 4 were waited for; matrix products, arithmetic and copies ran while one was open for 4% of the time, Pallas kernels for 0%

commit v1 on v0

--- a/solution.py
+++ b/solution.py
@@ -50,7 +50,11 @@
     values_new = qkv[:, 2 * width :]
     fresh = jnp.stack([keys_new, values_new])
     own_start = lax.axis_index("patch") * rows
-    whole = lax.all_gather(stale_kv[0], "patch", axis=1, tiled=True)
+    block = stale_kv[0]
+    size = lax.axis_size("patch")
+    shards = jnp.stack([block for _ in range(size)])
+    shards = lax.all_to_all(shards, "patch", split_axis=0, concat_axis=0)
+    whole = jnp.concatenate(shards, axis=1)
     whole = lax.dynamic_update_slice_in_dim(whole, fresh, own_start, 1)
     summed, top, total = partial_attention(queries, whole[0], whole[1])
     attended = (summed.reshape(rows, HEADS, HEAD_DIM) / total[..., None]).reshape(rows, width)

time: 267 us -> 231 us (0.87)
  the two profiles are of different devices: /device:TPU:2 before, /device:TPU:32 now
where the time goes in v1:
time: 231 us; the launch traced here: 230 us
  waiting for transfers between devices  174 us (75%)
  local copies, waits for them, and re-layouts  18.1 us (8%)
  between operations  14.2 us (6%)
  starting transfers between devices  8.49 us (4%)
  other arithmetic  8.07 us (3%)
  matrix products  7.76 us (3%)
    all_gather x1, waiting for transfers between devices, local(): lax.all_gather(normed, 'patch', axis=0, tiled=True)  81.3 us
    all_to_all x1, waiting for transfers between devices, local(): shards = lax.all_to_all(shards, 'patch', split_axis=0, concat_axis=0)  70.1 us
    all_to_all x1, waiting for transfers between devices, local(): lax.all_to_all(columns, 'patch', split_axis=0, concat_axis=1, tiled=True)  14.9 us
    ppermute x1, waiting for transfers between devices, from_behind(): lax.ppermute(shard, axis, [(i, (i + by) % count) for i in range(count)])  7.24 us
    another operation x1, local copies, waits for them, and re-layouts, local(): shards = jnp.stack([block for _ in range(size)])  5 us
    all_to_all x1, starting transfers between devices, local(): shards = lax.all_to_all(shards, 'patch', split_axis=0, concat_axis=0)  4.87 us
  transfers between devices with their start and end apart: 4, of which 4 were waited for; matrix products, arithmetic and copies ran while one was open for 2% of the time, Pallas kernels for 0%

profile of v1, /device:TPU:32, one launch (start us, length us, event | category | flops | bytes accessed | tf_op | source)
XLA Modules:
  0.0 230.2 jit_solution(3865955121033562802)
XLA Ops:
  7.2 0.0 copy-start
  7.2 0.0 all-gather.2.cloned.1.call-start
  7.2 0.8 reduce.1
  8.1 0.7 reduce.2
  8.8 1.2 fusion.23
  9.9 0.7 convert_bitcast_fusion.1
  10.6 2.0 fusion.26
  12.6 0.0 all-gather.2.cloned.1.call-update
  12.6 81.3 %all-gather.2.cloned.1.call-done = bf16[1024,1536]{1,0:T(8,128)(2,1)} async-done(((bf16[128,1536]{1,0:T(8,128)(2,1)}), bf16[1024,1536]{1,0:T(8,128)(2,1)}) %all-gather.2.cloned.1.call-update) | async-done | bytes 3145744 | tf_op jit(solution)/shard_map/all_gather | solution.py:43
  94.0 0.0 copy-done
  94.0 3.9 %fusion.12 = bf16[72,8,8,128]{3,2,1,0:T(8,128)(2,1)S(1)} fusion(bf16[1024,1536]{1,0:T(8,128)(2,1)} %all-gather.2.cloned.1.call-done, bf16[1,1536,576]{1,2,0:T(8,128)(2,1)S(1)} %copy-done), kind=kOutput, calls=%fused_computation.12 | convolution fusion | flops 1812529152 | bytes 6094848 | tf_op jit(solution)/shard_map/dot_general | solution.py:42
  97.9 1.2 copy.36
  99.1 3.6 %all-to-all-start.1 = ((bf16[8,128,576]{1,2,0:T(8,128)(2,1)}), bf16[8,128,576]{1,2,0:T(8,128)(2,1)S(1)}, u32[]{:S(2)}, u32[]{:S(2)}) async-start(bf16[8,128,576]{1,2,0:T(8,128)(2,1)} %bitcast.72), calls=%async_computation.1 | async-start | bytes 2359296 | tf_op jit(solution)/shard_map/all_to_all | solution.py:47
  102.7 2.3 copy.21
  105.0 14.9 %all-to-all-done.1 = bf16[8,128,576]{1,2,0:T(8,128)(2,1)S(1)} async-done(((bf16[8,128,576]{1,2,0:T(8,128)(2,1)}), bf16[8,128,576]{1,2,0:T(8,128)(2,1)S(1)}, u32[]{:S(2)}, u32[]{:S(2)}) %all-to-all-start.1) | async-done | bytes 1179680 | tf_op jit(solution)/shard_map/all_to_all | solution.py:47
  119.8 5.0 %stack.12 = bf16[8,2,128,1536]{2,3,1,0:T(8,128)(2,1)} broadcast(bf16[2,128,1536]{1,2,0:T(8,128)(2,1)} %copy.21), dimensions={1,2,3} | broadcast | bytes 7077888 | tf_op jit(solution)/shard_map/stack | solution.py:55
  124.8 4.9 %all-to-all-start = ((bf16[8,2,128,1536]{2,3,1,0:T(8,128)(2,1)}), bf16[8,2,128,1536]{2,3,1,0:T(8,128)(2,1)}, u32[]{:S(2)}, u32[]{:S(2)}) async-start(bf16[8,2,128,1536]{2,3,1,0:T(8,128)(2,1)} %stack.12), calls=%async_computation | async-start | bytes 12582912 | tf_op jit(solution)/shard_map/all_to_all | solution.py:56
  129.8 1.0 fusion.32
  130.7 70.1 %all-to-all-done = bf16[8,2,128,1536]{2,3,1,0:T(8,128)(2,1)} async-done(((bf16[8,2,128,1536]{2,3,1,0:T(8,128)(2,1)}), bf16[8,2,128,1536]{2,3,1,0:T(8,128)(2,1)}, u32[]{:S(2)}, u32[]{:S(2)}) %all-to-all-start) | async-done | bytes 6291488 | tf_op jit(solution)/shard_map/all_to_all | solution.py:56
  200.8 3.7 %copy_bitcast_fusion = bf16[2,1024,1536]{1,2,0:T(8,128)(2,1)S(1)} fusion(bf16[8,2,128,1536]{2,3,1,0:T(8,128)(2,1)} %all-to-all-done), kind=kLoop, calls=%fused_computation | loop fusion | bytes 12582912 | tf_op jit(solution)/shard_map/reshape | solution.py:57
  204.6 0.4 fusion.28
  205.0 0.7 fusion.31
  205.7 1.3 bitcast_reduce_fusion
  207.0 1.0 fusion.1
  208.1 0.0 copy-start.1
  208.1 2.6 %fusion.20 = f32[128,12,128]{0,2,1:T(8,128)} fusion(bf16[1024,12,128]{0,2,1:T(8,128)(2,1)S(1)} %bitcast.73, f32[12,1024,128]{2,1,0:T(8,128)S(1)} %get-tuple-element.14, f32[128,12]{0,1:T(8,128)S(1)} %get-tuple-element.13, f32[128,12]{0,1:T(8,128)S(1)} %fusion.1), kind=kOutput, calls=%fused_computation.19 | convolution fusion | flops 407568384 | bytes 10235904 | tf_op jit(solution)/shard_map/nht,thd->nhd/dot_general | solution.py:27
  210.6 2.3 copy.27
  212.9 1.2 fusion.27
  214.2 0.0 collective-permute-start
  214.2 1.2 copy.28
  215.3 7.2 %collective-permute-done = bf16[1,128,1536]{2,1,0:T(8,128)(2,1)S(1)} collective-permute-done((bf16[1,128,1536]{2,1,0:T(8,128)(2,1)S(1)}, bf16[1,128,1536]{2,1,0:T(8,128)(2,1)S(1)}, u32[]{:S(2)}, u32[]{:S(2)}) %collective-permute-start) | collective-permute-done | bytes 393248 | tf_op jit(solution)/shard_map/ppermute | solution.py:12
  222.6 0.7 copy.39
  (9 shorter events, 0.0 us)
Async XLA Ops:
  7.2 86.8 %copy-start = (bf16[1,1536,576]{1,2,0:T(8,128)(2,1)S(1)}, bf16[1,1536,576]{1,2,0:T(8,128)(2,1)}, u32[]{:S(2)}) copy-start(bf16[1,1536,576]{1,2,0:T(8,128)(2,1)} %param.8) | copy-start | bytes 5308420
  7.2 86.8 %all-gather.2.cloned.1.call-start = ((), (), s32[]{:S(2)}) async-start(), calls=%async_computation.2 | async-start | bytes 3538944 | tf_op jit(solution)/shard_map/all_gather | solution.py:43
  99.1 20.7 %all-to-all-start.1 = ((bf16[8,128,576]{1,2,0:T(8,128)(2,1)}), bf16[8,128,576]{1,2,0:T(8,128)(2,1)S(1)}, u32[]{:S(2)}, u32[]{:S(2)}) async-start(bf16[8,128,576]{1,2,0:T(8,128)(2,1)} %bitcast.72), calls=%async_computation.1 | async-start | bytes 2359296 | tf_op jit(solution)/shard_map/all_to_all | solution.py:47
  124.8 4.9 %copy-start.4 = (f32[1,1536]{1,0:T(1,128)S(1)}, f32[1,1536]{1,0:T(1,128)}, u32[]{:S(2)}) copy-start(f32[1,1536]{1,0:T(1,128)} %param.11) | copy-start | bytes 18436
  124.8 76.0 %all-to-all-start = ((bf16[8,2,128,1536]{2,3,1,0:T(8,128)(2,1)}), bf16[8,2,128,1536]{2,3,1,0:T(8,128)(2,1)}, u32[]{:S(2)}, u32[]{:S(2)}) async-start(bf16[8,2,128,1536]{2,3,1,0:T(8,128)(2,1)} %stack.12), calls=%async_computation | async-start | bytes 12582912 | tf_op jit(solution)/shard_map/all_to_all | solution.py:56
  130.7 73.9 %copy-start.2 = (bf16[1,128,1536]{1,2,0:T(8,128)(2,1)S(1)}, bf16[1,128,1536]{1,2,0:T(8,128)(2,1)}, u32[]{:S(2)}) copy-start(bf16[1,128,1536]{1,2,0:T(8,128)(2,1)} %get-tuple-element.9) | copy-start | bytes 1179652
  200.8 3.8 %copy-start.3 = (bf16[1,128,1536]{1,2,0:T(8,128)(2,1)S(1)}, bf16[1,128,1536]{1,2,0:T(8,128)(2,1)}, u32[]{:S(2)}) copy-start(bf16[1,128,1536]{1,2,0:T(8,128)(2,1)} %get-tuple-element.10) | copy-start | bytes 1179652
  208.1 4.9 %copy-start.1 = (bf16[1,128,1536]{2,1,0:T(8,128)(2,1)S(1)}, bf16[1,128,1536]{2,1,0:T(8,128)(2,1)}, u32[]{:S(2)}) copy-start(bf16[1,128,1536]{2,1,0:T(8,128)(2,1)} %param.7) | copy-start | bytes 1179652
  214.2 8.4 %collective-permute-start = (bf16[1,128,1536]{2,1,0:T(8,128)(2,1)S(1)}, bf16[1,128,1536]{2,1,0:T(8,128)(2,1)S(1)}, u32[]{:S(2)}, u32[]{:S(2)}) collective-permute-start(bf16[1,128,1536]{2,1,0:T(8,128)(2,1)S(1)} %fusion.27), channel_id=1, source_target_pairs={{0,8},{8,16},{16,24},{24,32},{32,40},{40,48},{48,56},{56,64},{64,7... | collective-permute-start | bytes 1179656 | tf_op jit(solution)/shard_map/ppermute | solution.py:12
Sparse Core Ops, SparseCore 0:
  12.7 81.1 all-gather.1
